TPU v7x, 256 devices: a whole 4x4x8 slice. The times are simulated.
256 devices in a mesh: src: 16 (over y, z_hi, core), tgt: 16 (over z_lo, x).
Axes of the slice: x: 4, y: 4, z: 8 (z_hi: 2, z_lo: 4; z = z_hi * 4 + z_lo), core: 2. Of those that a mesh axis runs over, the one named last changes fastest.
Arguments:
- source_points: float32 [64, 65536], P(None, ('src', 'tgt')), may hold values from -1.5 to 1.5
- target_points: float32 [64, 65536], P(None, ('src', 'tgt')), may hold values from -1.5 to 1.5
- source_logw: float32 [65536], P(('src', 'tgt')), may hold values from -2 to 2
- target_logw: float32 [65536], P(('src', 'tgt')), may hold values from -2 to 2
- potential_in: float32 [65536], P(('src', 'tgt')), may hold values from -5 to 61
- pair_list: int32 [256, 128, 2], P(('src', 'tgt')), may hold values from 0 to 255, as said below
- pair_counts: int32 [256], P(('src', 'tgt')), may hold values from 16 to 128, as said below
Outputs:
- source_potential: float32 [65536], P(('src', 'tgt'))
- target_potential: float32 [65536], P(('src', 'tgt'))
Inputs may be any that keep to these rules, and one draw needn't show every extreme that they name: `pair_list`: for row d = s * 16 + t, every source block lies in s * 16 to s * 16 + 15 and every target block equals t modulo 16; the entries of a row are distinct; only the first pair_counts[d] are live, later ones are ignored. Every source block and every target block whose ranges a row covers appears in a live pair of that row. `pair_counts`: some row has exactly 128 live pairs.
All inputs are finite; a program needn't handle non-finite values.
Results may differ from a plain program's by a relative error of at most 0.0003.
Values sent between devices are 32-bit elements; how exact they have to be, the bound alone decides.
No kernel may reach another device: no remote copies, remote signals or barrier semaphores. Data moves between devices by JAX's collectives and lax.ppermute only.
A program may use at most 64 MiB of HBM per device.

v0:
```python
import functools

import jax
import jax.numpy as jnp
from jax import lax
from jax.experimental import pallas as pl
from jax.experimental.pallas import tpu as pltpu
from jax.sharding import PartitionSpec as P

epsilon = 0.25
lowest_log = -1e30
log2e = 1.4426950408889634
ln2 = 0.6931471805599453
SIDE = 16
BLOCK = 256
FEAT = 64
ROWS = 72
UNROLL = 8
vmem_bytes = 24 * 1024 * 1024
full_tiles = 128


def merge_pair(first, second):
    highest = jnp.maximum(first[0], second[0])
    summed = first[1] * jnp.exp(first[0] - highest) + second[1] * jnp.exp(second[0] - highest)
    return (highest, summed)


def cross_cost(left_all, left_sq, row_id, right_all, right_sq, col_id, block_len):
    left_points = lax.dynamic_slice_in_dim(left_all, row_id * block_len, block_len, 1)
    right_points = lax.dynamic_slice_in_dim(right_all, col_id * block_len, block_len, 1)
    left_norm = lax.dynamic_slice_in_dim(left_sq, row_id * block_len, block_len, 0)
    right_norm = lax.dynamic_slice_in_dim(right_sq, col_id * block_len, block_len, 0)
    inner_prod = lax.dot_general(
        left_points,
        right_points,
        (((0,), (0,)), ((), ())),
        precision=lax.Precision.HIGHEST,
        preferred_element_type=jnp.float32,
    )
    return left_norm[:, None] + right_norm[None, :] - 2.0 * inner_prod


def fold_part(running, position, highest, summed):
    old_high = lax.dynamic_slice_in_dim(running[0], position, 1, 0)[0]
    old_sum = lax.dynamic_slice_in_dim(running[1], position, 1, 0)[0]
    new_high, new_sum = merge_pair((old_high, old_sum), (highest, summed))
    return (
        lax.dynamic_update_slice_in_dim(running[0], new_high[None, :], position, 0),
        lax.dynamic_update_slice_in_dim(running[1], new_sum[None, :], position, 0),
    )


def gather_blocks(points, axis):
    copies = jnp.broadcast_to(points, (lax.axis_size(axis), *points.shape))
    blocks = lax.all_to_all(copies, axis, 0, 0, tiled=True)
    return jnp.moveaxis(blocks, 0, 1).reshape(points.shape[0], -1)


def plain_form(
    source_points, target_points, source_logw, target_logw, potential_in, pair_list, pair_counts
):
    n_tgt = lax.axis_size("tgt")
    n_src = lax.axis_size("src")
    block_len = source_points.shape[1]
    group_points = gather_blocks(source_points, "tgt")
    group_logw = lax.all_gather(source_logw, "tgt", axis=0, tiled=True)
    column_points = gather_blocks(target_points, "src")
    column_g = lax.all_gather(potential_in, "src", axis=0, tiled=True)
    group_sq = jnp.sum(group_points * group_points, axis=0)
    column_sq = jnp.sum(column_points * column_points, axis=0)
    row_start = (
        jnp.full((n_tgt, block_len), lowest_log, dtype=jnp.float32),
        jnp.zeros((n_tgt, block_len), dtype=jnp.float32),
    )
    col_start = (
        jnp.full((n_src, block_len), lowest_log, dtype=jnp.float32),
        jnp.zeros((n_src, block_len), dtype=jnp.float32),
    )
    own_entries = pair_list[0]
    own_count = pair_counts[0]

    def row_visit_pair(slot_id, carry):
        row_id = own_entries[slot_id, 0] % n_tgt
        col_id = own_entries[slot_id, 1] // n_tgt
        tile_cost = cross_cost(
            group_points, group_sq, row_id, column_points, column_sq, col_id, block_len
        )
        g_piece = lax.dynamic_slice_in_dim(column_g, col_id * block_len, block_len, 0)
        scores = (g_piece[None, :] - tile_cost) / epsilon
        highest = jnp.max(scores, axis=1)
        summed = jnp.sum(jnp.exp(scores - highest[:, None]), axis=1)
        return fold_part(carry, row_id, highest, summed)

    row_parts = lax.fori_loop(0, own_count, row_visit_pair, row_start)
    row_high = lax.pmax(row_parts[0], "tgt")
    row_sum = lax.psum(row_parts[1] * jnp.exp(row_parts[0] - row_high), "tgt")
    f_group = epsilon * group_logw - epsilon * (row_high + jnp.log(row_sum)).reshape(-1)
    f_own = lax.dynamic_slice_in_dim(f_group, lax.axis_index("tgt") * block_len, block_len, 0)

    def col_visit_pair(slot_id, carry):
        row_id = own_entries[slot_id, 0] % n_tgt
        col_id = own_entries[slot_id, 1] // n_tgt
        tile_cost = cross_cost(
            group_points, group_sq, row_id, column_points, column_sq, col_id, block_len
        )
        f_piece = lax.dynamic_slice_in_dim(f_group, row_id * block_len, block_len, 0)
        scores = (f_piece[:, None] - tile_cost) / epsilon
        highest = jnp.max(scores, axis=0)
        summed = jnp.sum(jnp.exp(scores - highest[None, :]), axis=0)
        return fold_part(carry, col_id, highest, summed)

    col_parts = lax.fori_loop(0, own_count, col_visit_pair, col_start)
    col_high = lax.pmax(col_parts[0], "src")
    col_sum = lax.psum(col_parts[1] * jnp.exp(col_parts[0] - col_high), "src")
    own_high = lax.dynamic_slice_in_dim(col_high, lax.axis_index("src"), 1, 0)[0]
    own_sum = lax.dynamic_slice_in_dim(col_sum, lax.axis_index("src"), 1, 0)[0]
    g_own = epsilon * target_logw - epsilon * (own_high + jnp.log(own_sum))
    return (f_own, g_own)


vmem = pl.BlockSpec(memory_space=pltpu.VMEM)


def f32(*shape):
    return jax.ShapeDtypeStruct(shape, jnp.float32)


def pack_kernel(
    count_ref, ent_ref, x_ref, y_ref, lw_ref, g_ref, xp_ref, yp_ref, xsq_ref, ysq_ref, out_ref
):
    x = x_ref[...]
    y = y_ref[...]
    y_sq = jnp.sum(y * y, axis=0, keepdims=True)
    b = (4.0 * log2e) * (g_ref[...] - y_sq)
    row = lax.broadcasted_iota(jnp.int32, (8, BLOCK), 0)
    b_max = jnp.max(b, axis=1, keepdims=True)
    xp_ref[0:FEAT, :] = x
    xp_ref[FEAT:ROWS, :] = jnp.where(row == 0, lw_ref[...], b_max)
    yp_ref[0:FEAT, :] = y
    yp_ref[FEAT:ROWS, :] = jnp.broadcast_to(b, (8, BLOCK))
    xsq_ref[...] = jnp.sum(x * x, axis=0, keepdims=True)
    ysq_ref[...] = y_sq
    tgt_id, src_id, count = lax.axis_index("tgt"), lax.axis_index("src"), count_ref[...]
    my_z, my_x = tgt_id // 4, tgt_id % 4
    my_y, my_h, my_c = src_id // 4, (src_id // 2) % 2, src_id % 2
    lane = lax.broadcasted_iota(jnp.int32, (1, full_tiles), 1)
    live = lane < count

    def ordered(key, code):
        tall = jnp.broadcast_to(key, (full_tiles, full_tiles)).T
        rank = jnp.sum(jnp.where(tall < key, 1, 0), axis=0, keepdims=True)
        spot = jnp.broadcast_to(rank, (full_tiles, full_tiles)).T
        tall_code = jnp.broadcast_to(code, (full_tiles, full_tiles)).T
        return jnp.sum(jnp.where(spot == lane, tall_code, 0), axis=0, keepdims=True)

    def how_many(mask):
        return jnp.sum(jnp.where(mask, 1, 0), axis=1, keepdims=True)

    row = ent_ref[0:1, :] & 15
    col = ent_ref[1:2, :] >> 4
    q = (my_x - (row & 3)) & 3
    p = my_z ^ (row >> 2)
    h = ((col >> 1) & 1) ^ my_h
    c = (col & 1) ^ my_c
    turn = (my_y - (col >> 2)) & 3
    yat = (turn ^ (turn >> 1)) * 4 + c * 2 + h
    dy = (col >> 2) ^ my_y
    spot = h * 8 + c * 4 + (dy ^ (dy >> 1))
    stage = jnp.where(q == 2, 1, 0)
    code = row + spot * 16 + (q * 4 + p) * 256 + yat * 4096
    code = ordered(jnp.where(live, stage, 3) * 128 + lane, jnp.where(live, code, 0))
    far = (code & 128) != 0
    code_b = (code & 127) + lane * 256
    code_b = ordered(jnp.where(live, jnp.where(far, 0, 1), 2) * 128 + lane, code_b)
    out_ref[0:1, :] = code
    out_ref[1:2, :] = code_b
    first = how_many(live & (stage == 0))
    away = how_many(live & far)
    out_ref[2:3, :] = jnp.where(lane == 0, first, jnp.where(lane == 2, away, count))
    out_ref[3:8, :] = jnp.zeros((5, full_tiles), jnp.int32)


def pack(count, entries, x, y, lw, g):
    return pl.pallas_call(
        pack_kernel,
        out_shape=(
            pltpu.VMEM((ROWS, BLOCK), jnp.float32), pltpu.VMEM((ROWS, BLOCK), jnp.float32),
            pltpu.VMEM((1, BLOCK), jnp.float32), pltpu.VMEM((1, BLOCK), jnp.float32),
            pltpu.VMEM((8, full_tiles), jnp.int32),
        ),
        in_specs=[vmem] * 6,
        out_specs=[vmem] * 5,
        name="pack",
    )(count.reshape(1, 1), entries.T, x, y, lw.reshape(1, BLOCK), g.reshape(1, BLOCK))


def prepare_source(x, at, xa):
    x = x * (8.0 * log2e)
    hi = x.astype(jnp.bfloat16)
    lo = (x - hi.astype(jnp.float32)).astype(jnp.bfloat16)
    xa[at, 0:64, :] = hi
    xa[at, 64:128, :] = lo
    xa[at, 128:192, :] = hi
    xa[at, 192:256, :] = lo


def note_source(block, q, p, aux_ref):
    tgt_id = lax.axis_index("tgt")
    where = ((tgt_id // 4) ^ p) * 4 + ((tgt_id % 4 - q) & 3)
    mean = jnp.sum(block[0:FEAT], axis=1, keepdims=True) * (1.0 / BLOCK)
    aux_ref[pl.ds(where, 1), :] = block[FEAT : FEAT + 1]
    aux_ref[16:17, :] = jnp.maximum(aux_ref[16:17, :], block[FEAT + 1 : FEAT + 2])
    aux_ref[17:18, :] = jnp.maximum(aux_ref[17:18, :], jnp.sum(mean * mean, axis=0, keepdims=True))


def visit_tiles(unroll, plan_ref, begin, end, xa, ya, ub, k_ref, acc_ref):
    def group(step, carry):
        for u in range(unroll):
            raw = begin + step * unroll + u
            slot = jnp.minimum(raw, end - 1)
            code = plan_ref[0, slot]
            xat = (code >> 8) & 15
            yat = (code >> 12) & 15
            row = code & 15
            scores = jnp.dot(ya[yat], xa[xat], preferred_element_type=jnp.float32)
            tile = jnp.exp2(scores)
            k_ref[slot] = tile.astype(jnp.bfloat16)
            weight = ub[yat]
            left = jnp.sum((tile[:, 0:128] * weight).reshape(32, 8, 128), axis=0)
            right = jnp.sum((tile[:, 128:256] * weight).reshape(32, 8, 128), axis=0)
            live = raw < end
            acc_ref[row, :, 0:128] += jnp.where(live, left, 0.0)
            acc_ref[row, :, 128:256] += jnp.where(live, right, 0.0)
        return carry

    lax.fori_loop(0, pl.cdiv(end - begin, unroll), group, 0)


def first_kernel(
    plan_ref, x0, x1, x3, y0, z0, y1, z1, y2, z2, y3, z3,
    ya, ub, k_ref, acc_ref, aux_ref, stat_ref, xa, codes, sem,
):
    fetch = pltpu.make_async_copy(plan_ref, codes, sem)
    fetch.start()
    ys = (y0, z0, y1, z1, y2, z2, y3, z3)
    lines = [ys[at // 2][at % 2, FEAT : FEAT + 1, :] for at in range(SIDE)]
    top = jnp.max(functools.reduce(jnp.maximum, lines), axis=1, keepdims=True)
    low = jnp.min(functools.reduce(jnp.minimum, lines), axis=1, keepdims=True) - top
    y_sq = jnp.zeros((1, BLOCK), jnp.float32)
    for at in range(SIDE):
        y = ys[at // 2][at % 2, 0:FEAT, :]
        y_sq = jnp.maximum(y_sq, jnp.sum(y * y, axis=0, keepdims=True))
        turned = jnp.concatenate([y, y], axis=0).T
        hi = turned.astype(jnp.bfloat16)
        lo = (turned - hi.astype(jnp.float32)).astype(jnp.bfloat16)
        ya[at, :, 0:128] = hi
        ya[at, :, 128:256] = lo
        ub[at] = jnp.broadcast_to(jnp.exp2(lines[at] - top), (128, BLOCK)).T
    stat_ref[0:1, :] = jnp.broadcast_to(low, (1, BLOCK))
    stat_ref[1:2, :] = jnp.broadcast_to(top, (1, BLOCK))
    stat_ref[2:3, :] = y_sq
    stat_ref[3:8, :] = jnp.zeros((5, BLOCK), jnp.float32)
    aux_ref[0:16, :] = jnp.zeros((16, BLOCK), jnp.float32)
    aux_ref[16:17, :] = jnp.full((1, BLOCK), -1e30, jnp.float32)
    aux_ref[17:24, :] = jnp.zeros((7, BLOCK), jnp.float32)
    for q, ref in ((0, x0), (1, x1), (3, x3)):
        for p in range(4):
            block = ref[p]
            prepare_source(block[0:FEAT], q * 4 + p, xa)
            note_source(block, q, p, aux_ref)
    acc_ref[...] = jnp.zeros_like(acc_ref)
    fetch.wait()
    visit_tiles(2 * UNROLL, codes, 0, codes[2, 0], xa, ya, ub, k_ref, acc_ref)


def second_kernel(
    plan_ref, x2, ya, ub, k_in, acc_in, aux_in, stat_ref,
    k_ref, s_ref, aux_ref, xa, acc, codes, sem,
):
    fetch = pltpu.make_async_copy(plan_ref, codes, sem)
    fetch.start()
    aux_ref[...] = aux_in[...]
    acc[...] = acc_in[...]
    for p in range(4):
        block = x2[p]
        prepare_source(block[0:FEAT], 8 + p, xa)
        note_source(block, 2, p, aux_ref)
    fetch.wait()
    visit_tiles(UNROLL, codes, codes[2, 0], codes[2, 3], xa, ya, ub, k_ref, acc)
    total = jnp.sum(acc[...], axis=1)
    low = stat_ref[0:1, 0:1]
    top = stat_ref[1:2, 0:1]
    shift = aux_ref[16:17, 0:1]
    lean = (8.0 * log2e) * jnp.sqrt(aux_ref[17:18, 0:1] * jnp.max(stat_ref[2:3, :], axis=1, keepdims=True))
    most = jnp.max(jnp.max(total, axis=0, keepdims=True), axis=1, keepdims=True)
    apart = top - shift
    good = (
        (lean <= 24.0)
        & (low >= -105.0)
        & (jnp.abs(apart) <= 16.0)
        & (most <= jnp.exp2(120.0 + low))
    )
    s_ref[...] = jnp.where(good, total * jnp.exp2(apart), jnp.nan)
    aux_ref[18:19, :] = jnp.broadcast_to(apart, (1, BLOCK))


tiles_shape = pltpu.VMEM((full_tiles, BLOCK, BLOCK), jnp.bfloat16)
target_shape = pltpu.VMEM((SIDE, BLOCK, BLOCK), jnp.bfloat16)
weight_shape = pltpu.VMEM((SIDE, BLOCK, 128), jnp.float32)
row_cost = dict(flops=32 * 2 * BLOCK**3, bytes_accessed=1 << 20, transcendentals=32 * BLOCK * BLOCK)


codes_scratch = [pltpu.SMEM((8, full_tiles), jnp.int32), pltpu.SemaphoreType.DMA]


def source_scratch(blocks):
    return pltpu.VMEM((blocks, BLOCK, BLOCK), jnp.bfloat16)


def first_pass(order, xs, ys):
    return pl.pallas_call(
        first_kernel,
        out_shape=(
            target_shape, weight_shape, tiles_shape,
            f32(SIDE, 8, BLOCK), f32(24, BLOCK), f32(8, BLOCK),
        ),
        in_specs=[vmem] * 12,
        out_specs=[vmem] * 6,
        scratch_shapes=[source_scratch(SIDE), *codes_scratch],
        compiler_params=pltpu.CompilerParams(vmem_limit_bytes=vmem_bytes),
        cost_estimate=pl.CostEstimate(**row_cost),
        name="row_pass_a",
    )(order, *xs, *ys)


def second_pass(order, x2, ya, ub, tiles, acc, aux, stat):
    return pl.pallas_call(
        second_kernel,
        out_shape=(tiles_shape, f32(SIDE, BLOCK), f32(24, BLOCK)),
        in_specs=[vmem] * 8,
        out_specs=[vmem] * 3,
        scratch_shapes=[source_scratch(SIDE), pltpu.VMEM((SIDE, 8, BLOCK), jnp.float32), *codes_scratch],
        input_output_aliases={4: 0},
        compiler_params=pltpu.CompilerParams(vmem_limit_bytes=vmem_bytes),
        cost_estimate=pl.CostEstimate(**row_cost),
        name="row_pass_b",
    )(order, x2, ya, ub, tiles, acc, aux, stat)


def visit_columns(plan_ref, begin, end, v_ref, k_ref, t_ref, acc):
    acc[...] = jnp.zeros_like(acc)

    def group(step, carry):
        for u in range(UNROLL):
            raw = begin + step * UNROLL + u
            code = plan_ref[1, jnp.minimum(raw, end - 1)]
            v = jnp.where(raw < end, v_ref[pl.ds(code & 15, 1), :], 0.0)
            tile = k_ref[code >> 8].astype(jnp.float32)
            acc[(code >> 4) & 7] += tile[:, 0:128] * v[:, 0:128] + tile[:, 128:256] * v[:, 128:256]
        return carry

    lax.fori_loop(0, pl.cdiv(end - begin, UNROLL), group, 0)
    ones = jnp.ones((16, 128), jnp.bfloat16)
    across = (((1,), (1,)), ((), ()))
    for c in range(8):
        rest = acc[c]
        total = jnp.zeros((16, BLOCK), jnp.float32)
        for _ in range(3):
            part = rest.astype(jnp.bfloat16)
            rest = rest - part.astype(jnp.float32)
            total += lax.dot_general(ones, part, across, preferred_element_type=jnp.float32)
        t_ref[c : c + 1, :] = total[0:1, :]


def far_kernel(plan_ref, s_ref, aux_ref, xsq_ref, k_ref, f_ref, v_ref, t_ref, acc, codes, sem):
    fetch = pltpu.make_async_copy(plan_ref, codes, sem)
    fetch.start()
    total = s_ref[...]
    v = jnp.exp(aux_ref[0:16, :]) / total * jnp.exp2(aux_ref[18:19, :])
    fine = jnp.where((total >= 1.5e-11) & (total <= 4.3e12), 1.0, 0.0)
    fine = jnp.min(jnp.min(fine, axis=1, keepdims=True), axis=0, keepdims=True) > 0.5
    v_ref[...] = jnp.where(fine, v, jnp.nan)
    own = lax.axis_index("tgt")
    own_s = s_ref[pl.ds(own, 1), :]
    own_lw = aux_ref[pl.ds(own, 1), :]
    f_ref[...] = epsilon * own_lw - epsilon * (jnp.log(own_s) + ln2 * aux_ref[16:17, :]) + xsq_ref[...]
    fetch.wait()
    visit_columns(codes, 0, codes[2, 2], v_ref, k_ref, t_ref, acc)
    t_ref[...] += jnp.where(fine, 0.0, jnp.nan)


def near_kernel(plan_ref, v_ref, k_ref, t_ref, acc, codes, sem):
    fetch = pltpu.make_async_copy(plan_ref, codes, sem)
    fetch.start()
    fetch.wait()
    visit_columns(codes, codes[2, 2], codes[2, 3], v_ref, k_ref, t_ref, acc)


def far_pass(order, total, aux, xsq, tiles):
    return pl.pallas_call(
        far_kernel,
        out_shape=(f32(1, BLOCK), f32(SIDE, BLOCK), f32(8, BLOCK)),
        in_specs=[vmem] * 5,
        out_specs=[vmem] * 3,
        scratch_shapes=[pltpu.VMEM((8, BLOCK, 128), jnp.float32), *codes_scratch],
        compiler_params=pltpu.CompilerParams(vmem_limit_bytes=vmem_bytes),
        cost_estimate=pl.CostEstimate(**row_cost),
        name="col_pass_a",
    )(order, total, aux, xsq, tiles)


def near_pass(order, v, tiles):
    return pl.pallas_call(
        near_kernel,
        out_shape=f32(8, BLOCK),
        in_specs=[vmem] * 3,
        out_specs=vmem,
        scratch_shapes=[pltpu.VMEM((8, BLOCK, 128), jnp.float32), *codes_scratch],
        compiler_params=pltpu.CompilerParams(vmem_limit_bytes=vmem_bytes),
        cost_estimate=pl.CostEstimate(**row_cost),
        name="col_pass_b",
    )(order, v, tiles)


def ring(k):
    return [(i, (i // 4) * 4 + (i + k) % 4) for i in range(SIDE)]


def hop(k):
    return [(i, (i + 4 * k) % SIDE) for i in range(SIDE)]


def swap(bits):
    return [(i, i ^ bits) for i in range(SIDE)]


def fast_form(x, y, lw, g, entries, count):
    xp, yp, x_sq, y_sq, order = pack(count, entries, x, y, lw, g)
    xz = jnp.stack([xp] + [lax.ppermute(xp, "tgt", swap(4 * k)) for k in (1, 2, 3)])
    yh = jnp.stack([yp, lax.ppermute(yp, "src", swap(2))])
    x1 = lax.ppermute(xz, "tgt", ring(1))
    x3 = lax.ppermute(xz, "tgt", ring(3))
    yy = [yh] + [lax.ppermute(yh, "src", hop(k)) for k in (1, 3, 2)]
    x2 = lax.ppermute(x1, "tgt", ring(1))
    ys = [z for a in yy for z in (a, lax.ppermute(a, "src", swap(1)))]

    ya, ub, tiles, acc, aux, stat = first_pass(order, (xz, x1, x3), ys)
    tiles, total, aux = second_pass(order, x2, ya, ub, tiles, acc, aux, stat)

    one, two, three = [lax.ppermute(total, "tgt", swap(k)) for k in (1, 2, 3)]
    total = (three + one) + (total + two)
    one, two, three = [lax.ppermute(total, "tgt", swap(4 * k)) for k in (1, 2, 3)]
    total = (one + two) + (total + three)

    f_own, v, away = far_pass(order, total, aux, x_sq, tiles)
    from_far = lax.ppermute(away, "src", swap(2))
    part = near_pass(order, v, tiles) + from_far
    part = part[0:4] + lax.ppermute(part[4:8], "src", swap(1))
    one, other, across = [
        lax.ppermute(part[k : k + 1], "src", swap(bits)) for k, bits in ((1, 4), (2, 12), (3, 8))
    ]
    part = (other + one) + (part[0:1] + across)
    offset = epsilon * ln2 * stat[1] + y_sq.reshape(BLOCK)
    return f_own.reshape(BLOCK), part.reshape(BLOCK), offset


def on_device(
    source_points, target_points, source_logw, target_logw, potential_in, pair_list, pair_counts
):
    f_own, t_own, offset = fast_form(
        source_points, target_points, source_logw, potential_in, pair_list[0], pair_counts
    )
    g_own = epsilon * target_logw - epsilon * jnp.log(t_own) + offset
    out_of_range = jnp.isnan(t_own[0])
    return lax.cond(
        out_of_range,
        plain_form,
        lambda *_: (f_own, g_own),
        source_points, target_points, source_logw, target_logw, potential_in, pair_list, pair_counts,
    )


def solution(mesh):
    return jax.shard_map(
        on_device,
        mesh=mesh,
        in_specs=(
            P(None, ("src", "tgt")),
            P(None, ("src", "tgt")),
            P(("src", "tgt")),
            P(("src", "tgt")),
            P(("src", "tgt")),
            P(("src", "tgt"), None, None),
            P(("src", "tgt")),
        ),
        out_specs=(P(("src", "tgt")), P(("src", "tgt"))),
        check_vma=False,
    )
```

profile of v0, /device:TPU:0, one launch (start us, length us, event | category | flops | bytes accessed | tf_op | source)
XLA Modules:
  0.0 2187.6 jit_solution(14348708813982370955)
XLA Ops:
  1.3 1.5 pack.1
  2.8 3.0 collective-permute-start.2
  7.2 5.5 collective-permute-start.6
  12.7 1.6 collective-permute-start.3
  14.3 3.6 collective-permute-done.6
  17.9 3.3 collective-permute-start.12
  23.2 2.1 collective-permute-done.12.y3
  25.3 2.8 collective-permute-start.5
  30.2 2.7 collective-permute-done.5.x3
  32.9 5.3 row_pass_a.1
  38.2 2.3 row_pass_b.1
  40.6 2.5 collective-permute-start.16
  43.1 2.1 collective-permute-start.15
  45.2 2.6 collective-permute-start.14
  47.8 2.4 collective-permute-done.14
  50.3 2.9 collective-permute-start.18
  57.0 2.5 col_pass_a.1
  59.5 6.3 collective-permute-start.20
  65.8 2.7 col_pass_b.1
  70.7 2.8 collective-permute-start.24
  75.7 2.6 collective-permute-done.22
  80.2 2107.4 %conditional.1 = (f32[256]{0:T(256)}, f32[256]{0:T(256)}) conditional(s32[]{:T(128)} %bitcast.31, (f32[1,256]{1,0:T(1,128)}, f32[256]{0:T(256)S(1)}, f32[1,256]{1,0:T(1,128)S(1)}, f32[8,256]{1,0:T(8,128)S(1)}, f32[1,256]{1,0:T(1,128)S(1)}) %tuple.111, (f32[256]{0:T(256)S(1)}, s32[1]{0:T(128)}, s32[1,128,2]{1,2,0:T(2,128)S(1)}, ...), branch_computations={%region_0.0_spmd, %region_1.16_spmd} | conditional | flops 102804560 | bytes 15752996 | solution.py:476
  80.3 28.6 %all_to_all.8 = f32[16,64,256]{2,1,0:T(8,128)S(1)} all-to-all(f32[16,64,256]{2,1,0:T(8,128)S(1)} %broadcast_in_dim.0), channel_id=1, replica_groups=mesh['src'=16,'tgt'=16] {'tgt'}, dimensions={0} | all-to-all | bytes 2097152 | tf_op jit(solution)/shard_map/cond/branch_1_fun/all_to_all | solution.py:56
  109.9 6.7 all-to-all-start.1
  116.7 52.0 %all-gather = f32[16,1,256]{2,1,0:T(1,128)S(1)} all-gather(f32[1,1,256]{2,1,0:T(1,128)S(1)} %bitcast.91), channel_id=1, replica_groups=mesh['src'=16,'tgt'=16] {'tgt'}, dimensions={0}, use_global_device_ids=true | all-gather | bytes 17408 | tf_op jit(solution)/shard_map/cond/branch_1_fun/all_gather | solution.py:67
  168.7 31.6 %all-gather.1 = f32[16,1,256]{2,1,0:T(1,128)S(1)} all-gather(f32[1,1,256]{2,1,0:T(1,128)S(1)} %bitcast.93), channel_id=1, replica_groups=mesh['src'=16,'tgt'=16] {'src'}, dimensions={0}, use_global_device_ids=true | all-gather | bytes 17408 | tf_op jit(solution)/shard_map/cond/branch_1_fun/all_gather | solution.py:69
  200.8 498.7 %while.26 = (s32[]{:T(128)}, f32[16,256]{1,0:T(8,128)S(1)}, f32[16,256]{1,0:T(8,128)S(1)}, s32[]{:T(128)}, s32[128,2]{0,1:T(2,128)S(1)}, /*index=5*/f32[4096]{0:...) while((s32[]{:T(128)}, f32[16,256]{1,0:T(8,128)S(1)}, ...), condition=%wide.region_7.7_spmd, body=%wide.region_4.6_spmd.sunk | while | flops 50857000 | bytes 678540 | solution.py:95
  699.5 404.0 %pmax.12 = f32[16,256]{1,0:T(8,128)S(1)} all-reduce(f32[16,256]{1,0:T(8,128)S(1)} %get-tuple-element.314), channel_id=1, replica_groups=mesh['src'=16,'tgt'=16] {'tgt'}, use_global_device_ids=true, to_apply=%region_8.8 | all-reduce | flops 4096 | bytes 32768 | tf_op jit(solution)/shard_map/cond/branch_1_fun/pmax | solution.py:96
  1103.5 74.2 %psum.12 = f32[16,256]{1,0:T(8,128)S(1)} all-reduce(f32[16,256]{1,0:T(8,128)S(1)} %exponential_multiply_fusion.1), channel_id=1, replica_groups=mesh['src'=16,'tgt'=16] {'tgt'}, use_global_device_ids=true, to_apply=%region_9.9 | all-reduce | flops 4096 | bytes 32768 | tf_op jit(solution)/shard_map/cond/branch_1_fun/psum | solution.py:97
  1177.8 498.6 %while.27 = (s32[]{:T(128)}, f32[16,256]{1,0:T(8,128)S(1)}, f32[16,256]{1,0:T(8,128)S(1)}, s32[]{:T(128)}, s32[128,2]{0,1:T(2,128)S(1)}, /*index=5*/f32[4096]{0:...) while((s32[]{:T(128)}, f32[16,256]{1,0:T(8,128)S(1)}, ...), condition=%wide.region_13.13_spmd, body=%wide.region_10.12_spmd.sunk | while | flops 50857000 | bytes 678540 | solution.py:113
  1677.0 425.8 %pmax.13 = f32[16,256]{1,0:T(8,128)S(1)} all-reduce(f32[16,256]{1,0:T(8,128)S(1)} %get-tuple-element.317), channel_id=1, replica_groups=mesh['src'=16,'tgt'=16] {'src'}, use_global_device_ids=true, to_apply=%region_14.14 | all-reduce | flops 4096 | bytes 32768 | tf_op jit(solution)/shard_map/cond/branch_1_fun/pmax | solution.py:114
  2102.8 84.1 %psum.13 = f32[16,256]{1,0:T(8,128)S(1)} all-reduce(f32[16,256]{1,0:T(8,128)S(1)} %exponential_multiply_fusion), channel_id=1, replica_groups=mesh['src'=16,'tgt'=16] {'src'}, use_global_device_ids=true, to_apply=%region_15.15 | all-reduce | flops 4096 | bytes 32768 | tf_op jit(solution)/shard_map/cond/branch_1_fun/psum | solution.py:115
  (1446 shorter events, 247.7 us)
Async XLA Ops:
  2.8 9.9 collective-permute-start.2
  5.7 7.0 collective-permute-start.1
  5.7 7.0 collective-permute-start
  7.2 10.6 collective-permute-start.6
  12.7 15.3 collective-permute-start.3
  17.9 7.4 collective-permute-start.12
  21.2 6.9 collective-permute-start.10
  22.2 6.4 collective-permute-start.8
  23.2 5.5 collective-permute-start.7
  25.3 7.6 collective-permute-start.5
  28.1 10.1 collective-permute-start.4
  28.1 1.5 collective-permute-start.13
  28.6 1.4 collective-permute-start.11
  28.7 1.5 collective-permute-start.9
  40.6 7.2 collective-permute-start.16
  43.1 4.7 collective-permute-start.15
  45.2 4.9 collective-permute-start.14
  50.2 5.8 collective-permute-start.19
  50.3 5.7 collective-permute-start.18
  53.2 3.7 collective-permute-start.17
  56.9 23.2 %copy-start = (f32[64,256]{1,0:T(8,128)S(1)}, f32[64,256]{1,0:T(8,128)}, u32[]{:S(2)}) copy-start(f32[64,256]{1,0:T(8,128)} %x_ref.1) | copy-start | bytes 196612
  56.9 23.2 %copy-start.1 = (f32[64,256]{1,0:T(8,128)S(1)}, f32[64,256]{1,0:T(8,128)}, u32[]{:S(2)}) copy-start(f32[64,256]{1,0:T(8,128)} %y_ref.1) | copy-start | bytes 196612
  56.9 23.2 %copy-start.2 = (s32[1,128,2]{1,2,0:T(2,128)S(1)}, s32[1,128,2]{1,2,0:T(2,128)}, u32[]{:S(2)}) copy-start(s32[1,128,2]{1,2,0:T(2,128)} %param.18) | copy-start | bytes 3076
  56.9 23.2 %copy-start.3 = (f32[256]{0:T(256)S(1)}, f32[256]{0:T(256)}, u32[]{:S(2)}) copy-start(f32[256]{0:T(256)} %param.15) | copy-start | bytes 3076
  56.9 23.2 %copy-start.4 = (f32[256]{0:T(256)S(1)}, f32[256]{0:T(256)}, u32[]{:S(2)}) copy-start(f32[256]{0:T(256)} %param.17) | copy-start | bytes 3076
  57.0 23.2 %copy-start.5 = (f32[256]{0:T(256)S(1)}, f32[256]{0:T(256)}, u32[]{:S(2)}) copy-start(f32[256]{0:T(256)} %param.16) | copy-start | bytes 3076
  59.5 9.0 collective-permute-start.20
  68.5 1.3 collective-permute-start.21
  69.8 4.8 collective-permute-start.23
  70.7 5.1 collective-permute-start.24
  73.5 4.8 collective-permute-start.22
  109.9 90.6 %all-to-all-start.1 = ((f32[16,64,256]{2,1,0:T(8,128)}), f32[16,64,256]{2,1,0:T(8,128)S(1)}, u32[]{:S(2)}, u32[]{:S(2)}) async-start(f32[16,64,256]{2,1,0:T(8,128)} %broadcast_in_dim.1), calls=%async_computation.1 | async-start | bytes 2097152 | tf_op jit(solution)/shard_map/cond/branch_1_fun/all_to_all | solution.py:56
where the time goes:
time: 2200 us; the launch traced here: 2190 us
  blocking collectives  1100 us (50%)
  loops' own time  767 us (35%)
  local copies, waits for them, and re-layouts  151 us (7%)
  matrix products  67.8 us (3%)
  starting transfers between devices  49.8 us (2%)
    pmax x1, blocking collectives, plain_form(): col_high = lax.pmax(col_parts[0], 'src')  426 us
    pmax x1, blocking collectives, plain_form(): row_high = lax.pmax(row_parts[0], 'tgt')  404 us
    another operation x1, loops' own time, plain_form(): col_parts = lax.fori_loop(0, own_count, col_visit_pair, col_start)  383 us
    another operation x1, loops' own time, plain_form(): row_parts = lax.fori_loop(0, own_count, row_visit_pair, row_start)  383 us
    psum x1, blocking collectives, plain_form(): col_sum = lax.psum(col_parts[1] * jnp.exp(col_parts[0] - col_high), 'src')  84.1 us
    psum x1, blocking collectives, plain_form(): row_sum = lax.psum(row_parts[1] * jnp.exp(row_parts[0] - row_high), 'tgt')  74.2 us
    dot_general x152, matrix products, cross_cost(): lax.dot_general(left_points, right_points, (((0,), (0,)), ((), ())), prec...  67.8 us
    all_gather x1, blocking collectives, plain_form(): group_logw = lax.all_gather(source_logw, 'tgt', axis=0, tiled=True)  52 us
  transfers between devices with their start and end apart: 26, of which 13 were waited for; matrix products, arithmetic and copies ran while one was open for 0% of the time, Pallas kernels for 0%

commit v1 on v0

--- a/solution.py
+++ b/solution.py
@@ -127,16 +127,14 @@
 
 
 def pack_kernel(
-    count_ref, ent_ref, x_ref, y_ref, lw_ref, g_ref, xp_ref, yp_ref, xsq_ref, ysq_ref, out_ref
+    count_ref, ent_ref, x_ref, y_ref, g_ref, lw_ref, yp_ref, xv_ref, xsq_ref, ysq_ref, lwv_ref, out_ref
 ):
     x = x_ref[...]
+    xv_ref[...] = x
+    lwv_ref[...] = lw_ref[...]
     y = y_ref[...]
     y_sq = jnp.sum(y * y, axis=0, keepdims=True)
     b = (4.0 * log2e) * (g_ref[...] - y_sq)
-    row = lax.broadcasted_iota(jnp.int32, (8, BLOCK), 0)
-    b_max = jnp.max(b, axis=1, keepdims=True)
-    xp_ref[0:FEAT, :] = x
-    xp_ref[FEAT:ROWS, :] = jnp.where(row == 0, lw_ref[...], b_max)
     yp_ref[0:FEAT, :] = y
     yp_ref[FEAT:ROWS, :] = jnp.broadcast_to(b, (8, BLOCK))
     xsq_ref[...] = jnp.sum(x * x, axis=0, keepdims=True)
@@ -181,18 +179,18 @@
     out_ref[3:8, :] = jnp.zeros((5, full_tiles), jnp.int32)
 
 
-def pack(count, entries, x, y, lw, g):
+def pack(count, entries, x, y, g, lw):
     return pl.pallas_call(
         pack_kernel,
         out_shape=(
-            pltpu.VMEM((ROWS, BLOCK), jnp.float32), pltpu.VMEM((ROWS, BLOCK), jnp.float32),
-            pltpu.VMEM((1, BLOCK), jnp.float32), pltpu.VMEM((1, BLOCK), jnp.float32),
+            pltpu.VMEM((ROWS, BLOCK), jnp.float32), pltpu.VMEM((FEAT, BLOCK), jnp.float32),
+            pltpu.VMEM((1, BLOCK), jnp.float32), pltpu.VMEM((1, BLOCK), jnp.float32), pltpu.VMEM((1, BLOCK), jnp.float32),
             pltpu.VMEM((8, full_tiles), jnp.int32),
         ),
         in_specs=[vmem] * 6,
-        out_specs=[vmem] * 5,
+        out_specs=[vmem] * 6,
         name="pack",
-    )(count.reshape(1, 1), entries.T, x, y, lw.reshape(1, BLOCK), g.reshape(1, BLOCK))
+    )(count.reshape(1, 1), entries.T, x, y, g.reshape(1, BLOCK), lw.reshape(1, BLOCK))
 
 
 def prepare_source(x, at, xa):
@@ -205,13 +203,9 @@
     xa[at, 192:256, :] = lo
 
 
-def note_source(block, q, p, aux_ref):
-    tgt_id = lax.axis_index("tgt")
-    where = ((tgt_id // 4) ^ p) * 4 + ((tgt_id % 4 - q) & 3)
-    mean = jnp.sum(block[0:FEAT], axis=1, keepdims=True) * (1.0 / BLOCK)
-    aux_ref[pl.ds(where, 1), :] = block[FEAT : FEAT + 1]
-    aux_ref[16:17, :] = jnp.maximum(aux_ref[16:17, :], block[FEAT + 1 : FEAT + 2])
-    aux_ref[17:18, :] = jnp.maximum(aux_ref[17:18, :], jnp.sum(mean * mean, axis=0, keepdims=True))
+def mean_square(block):
+    mean = jnp.sum(block, axis=1, keepdims=True) * (1.0 / BLOCK)
+    return jnp.sum(mean * mean, axis=0, keepdims=True)
 
 
 def visit_tiles(unroll, plan_ref, begin, end, xa, ya, ub, k_ref, acc_ref):
@@ -239,7 +233,7 @@
 
 def first_kernel(
     plan_ref, x0, x1, x3, y0, z0, y1, z1, y2, z2, y3, z3,
-    ya, ub, k_ref, acc_ref, aux_ref, stat_ref, xa, codes, sem,
+    ya, ub, k_ref, acc_ref, stat_ref, xa, codes, sem,
 ):
     fetch = pltpu.make_async_copy(plan_ref, codes, sem)
     fetch.start()
@@ -260,49 +254,42 @@
     stat_ref[0:1, :] = jnp.broadcast_to(low, (1, BLOCK))
     stat_ref[1:2, :] = jnp.broadcast_to(top, (1, BLOCK))
     stat_ref[2:3, :] = y_sq
-    stat_ref[3:8, :] = jnp.zeros((5, BLOCK), jnp.float32)
-    aux_ref[0:16, :] = jnp.zeros((16, BLOCK), jnp.float32)
-    aux_ref[16:17, :] = jnp.full((1, BLOCK), -1e30, jnp.float32)
-    aux_ref[17:24, :] = jnp.zeros((7, BLOCK), jnp.float32)
+    x_mean = jnp.zeros((1, 1), jnp.float32)
     for q, ref in ((0, x0), (1, x1), (3, x3)):
         for p in range(4):
             block = ref[p]
-            prepare_source(block[0:FEAT], q * 4 + p, xa)
-            note_source(block, q, p, aux_ref)
+            prepare_source(block, q * 4 + p, xa)
+            x_mean = jnp.maximum(x_mean, mean_square(block))
+    stat_ref[3:4, :] = jnp.broadcast_to(x_mean, (1, BLOCK))
+    stat_ref[4:8, :] = jnp.zeros((4, BLOCK), jnp.float32)
     acc_ref[...] = jnp.zeros_like(acc_ref)
     fetch.wait()
     visit_tiles(2 * UNROLL, codes, 0, codes[2, 0], xa, ya, ub, k_ref, acc_ref)
 
 
 def second_kernel(
-    plan_ref, x2, ya, ub, k_in, acc_in, aux_in, stat_ref,
-    k_ref, s_ref, aux_ref, xa, acc, codes, sem,
+    plan_ref, x2, ya, ub, k_in, acc_in, stat_ref, lw_ref, k_ref, s_ref, xa, acc, codes, sem
 ):
     fetch = pltpu.make_async_copy(plan_ref, codes, sem)
     fetch.start()
-    aux_ref[...] = aux_in[...]
     acc[...] = acc_in[...]
+    x_mean = stat_ref[3:4, 0:1]
     for p in range(4):
         block = x2[p]
-        prepare_source(block[0:FEAT], 8 + p, xa)
-        note_source(block, 2, p, aux_ref)
+        prepare_source(block, 8 + p, xa)
+        x_mean = jnp.maximum(x_mean, mean_square(block))
     fetch.wait()
     visit_tiles(UNROLL, codes, codes[2, 0], codes[2, 3], xa, ya, ub, k_ref, acc)
     total = jnp.sum(acc[...], axis=1)
     low = stat_ref[0:1, 0:1]
-    top = stat_ref[1:2, 0:1]
-    shift = aux_ref[16:17, 0:1]
-    lean = (8.0 * log2e) * jnp.sqrt(aux_ref[17:18, 0:1] * jnp.max(stat_ref[2:3, :], axis=1, keepdims=True))
+    lean = (8.0 * log2e) * jnp.sqrt(x_mean * jnp.max(stat_ref[2:3, :], axis=1, keepdims=True))
     most = jnp.max(jnp.max(total, axis=0, keepdims=True), axis=1, keepdims=True)
-    apart = top - shift
-    good = (
-        (lean <= 24.0)
-        & (low >= -105.0)
-        & (jnp.abs(apart) <= 16.0)
-        & (most <= jnp.exp2(120.0 + low))
-    )
-    s_ref[...] = jnp.where(good, total * jnp.exp2(apart), jnp.nan)
-    aux_ref[18:19, :] = jnp.broadcast_to(apart, (1, BLOCK))
+    good = (lean <= 24.0) & (low >= -105.0) & (most <= jnp.exp2(120.0 + low))
+    s_ref[0:16, :] = jnp.where(good, total, jnp.nan)
+    s_ref[16:17, :] = stat_ref[1:2, :]
+    s_ref[17:18, :] = stat_ref[1:2, :]
+    s_ref[18:19, :] = lw_ref[...]
+    s_ref[19:24, :] = jnp.zeros((5, BLOCK), jnp.float32)
 
 
 tiles_shape = pltpu.VMEM((full_tiles, BLOCK, BLOCK), jnp.bfloat16)
@@ -323,10 +310,10 @@
         first_kernel,
         out_shape=(
             target_shape, weight_shape, tiles_shape,
-            f32(SIDE, 8, BLOCK), f32(24, BLOCK), f32(8, BLOCK),
+            f32(SIDE, 8, BLOCK), f32(8, BLOCK),
         ),
         in_specs=[vmem] * 12,
-        out_specs=[vmem] * 6,
+        out_specs=[vmem] * 5,
         scratch_shapes=[source_scratch(SIDE), *codes_scratch],
         compiler_params=pltpu.CompilerParams(vmem_limit_bytes=vmem_bytes),
         cost_estimate=pl.CostEstimate(**row_cost),
@@ -334,18 +321,18 @@
     )(order, *xs, *ys)
 
 
-def second_pass(order, x2, ya, ub, tiles, acc, aux, stat):
+def second_pass(order, x2, ya, ub, tiles, acc, stat, lw):
     return pl.pallas_call(
         second_kernel,
-        out_shape=(tiles_shape, f32(SIDE, BLOCK), f32(24, BLOCK)),
+        out_shape=(tiles_shape, f32(24, BLOCK)),
         in_specs=[vmem] * 8,
-        out_specs=[vmem] * 3,
+        out_specs=[vmem] * 2,
         scratch_shapes=[source_scratch(SIDE), pltpu.VMEM((SIDE, 8, BLOCK), jnp.float32), *codes_scratch],
         input_output_aliases={4: 0},
         compiler_params=pltpu.CompilerParams(vmem_limit_bytes=vmem_bytes),
         cost_estimate=pl.CostEstimate(**row_cost),
         name="row_pass_b",
-    )(order, x2, ya, ub, tiles, acc, aux, stat)
+    )(order, x2, ya, ub, tiles, acc, stat, lw)
 
 
 def visit_columns(plan_ref, begin, end, v_ref, k_ref, t_ref, acc):
@@ -373,18 +360,24 @@
         t_ref[c : c + 1, :] = total[0:1, :]
 
 
-def far_kernel(plan_ref, s_ref, aux_ref, xsq_ref, k_ref, f_ref, v_ref, t_ref, acc, codes, sem):
+def far_kernel(
+    plan_ref, s_ref, ends_ref, lw_ref, stat_ref, xsq_ref, k_ref, f_ref, v_ref, t_ref, acc, codes, sem
+):
     fetch = pltpu.make_async_copy(plan_ref, codes, sem)
     fetch.start()
     total = s_ref[...]
-    v = jnp.exp(aux_ref[0:16, :]) / total * jnp.exp2(aux_ref[18:19, :])
-    fine = jnp.where((total >= 1.5e-11) & (total <= 4.3e12), 1.0, 0.0)
+    shift = ends_ref[0:1, :]
+    own = lax.axis_index("tgt")
+    for r in range(SIDE):
+        off = (r // 4) * 4 + (0, 3, 1, 2)[r % 4]
+        v_ref[pl.ds(own ^ off, 1), :] = lw_ref[r : r + 1, :]
+    v = jnp.exp(v_ref[...]) / total * jnp.exp2(stat_ref[1:2, :] - shift)
+    fine = (total >= 1.5e-11) & (total <= 4.3e12) & (shift - ends_ref[1:2, :] <= 16.0)
+    fine = jnp.where(fine, 1.0, 0.0)
     fine = jnp.min(jnp.min(fine, axis=1, keepdims=True), axis=0, keepdims=True) > 0.5
     v_ref[...] = jnp.where(fine, v, jnp.nan)
-    own = lax.axis_index("tgt")
     own_s = s_ref[pl.ds(own, 1), :]
-    own_lw = aux_ref[pl.ds(own, 1), :]
-    f_ref[...] = epsilon * own_lw - epsilon * (jnp.log(own_s) + ln2 * aux_ref[16:17, :]) + xsq_ref[...]
+    f_ref[...] = epsilon * lw_ref[0:1, :] - epsilon * (jnp.log(own_s) + ln2 * shift) + xsq_ref[...]
     fetch.wait()
     visit_columns(codes, 0, codes[2, 2], v_ref, k_ref, t_ref, acc)
     t_ref[...] += jnp.where(fine, 0.0, jnp.nan)
@@ -397,17 +390,17 @@
     visit_columns(codes, codes[2, 2], codes[2, 3], v_ref, k_ref, t_ref, acc)
 
 
-def far_pass(order, total, aux, xsq, tiles):
+def far_pass(order, total, ends, lw, stat, xsq, tiles):
     return pl.pallas_call(
         far_kernel,
         out_shape=(f32(1, BLOCK), f32(SIDE, BLOCK), f32(8, BLOCK)),
-        in_specs=[vmem] * 5,
+        in_specs=[vmem] * 7,
         out_specs=[vmem] * 3,
         scratch_shapes=[pltpu.VMEM((8, BLOCK, 128), jnp.float32), *codes_scratch],
         compiler_params=pltpu.CompilerParams(vmem_limit_bytes=vmem_bytes),
         cost_estimate=pl.CostEstimate(**row_cost),
         name="col_pass_a",
-    )(order, total, aux, xsq, tiles)
+    )(order, total, ends, lw, stat, xsq, tiles)
 
 
 def near_pass(order, v, tiles):
@@ -435,9 +428,26 @@
     return [(i, i ^ bits) for i in range(SIDE)]
 
 
+def stacked(rows, *pieces):
+    out, at = 0.0, 0
+    for piece in pieces:
+        height = piece.shape[0]
+        out = out + lax.pad(piece, jnp.float32(0.0), ((at, rows - at - height, 0), (0, 0, 0)))
+        at += height
+    return out
+
+
+def one_scale(*parts_weights):
+    *parts, weights = parts_weights
+    high = functools.reduce(jnp.maximum, [p[16:17] for p in parts])
+    low = functools.reduce(jnp.minimum, [p[17:18] for p in parts])
+    scaled = lax.optimization_barrier([p[0:16] * jnp.exp2(p[16:17] - high) for p in parts])
+    return scaled, stacked(2, high, low), stacked(4 * weights, *[p[18 : 18 + weights] for p in parts])
+
+
 def fast_form(x, y, lw, g, entries, count):
-    xp, yp, x_sq, y_sq, order = pack(count, entries, x, y, lw, g)
-    xz = jnp.stack([xp] + [lax.ppermute(xp, "tgt", swap(4 * k)) for k in (1, 2, 3)])
+    yp, own_x, x_sq, y_sq, lw, order = pack(count, entries, x, y, g, lw)
+    xz = jnp.stack([own_x] + [lax.ppermute(x, "tgt", swap(4 * k)) for k in (1, 2, 3)])
     yh = jnp.stack([yp, lax.ppermute(yp, "src", swap(2))])
     x1 = lax.ppermute(xz, "tgt", ring(1))
     x3 = lax.ppermute(xz, "tgt", ring(3))
@@ -445,15 +455,17 @@
     x2 = lax.ppermute(x1, "tgt", ring(1))
     ys = [z for a in yy for z in (a, lax.ppermute(a, "src", swap(1)))]
 
-    ya, ub, tiles, acc, aux, stat = first_pass(order, (xz, x1, x3), ys)
-    tiles, total, aux = second_pass(order, x2, ya, ub, tiles, acc, aux, stat)
+    ya, ub, tiles, acc, stat = first_pass(order, (xz, x1, x3), ys)
+    tiles, total = second_pass(order, x2, ya, ub, tiles, acc, stat, lw)
 
     one, two, three = [lax.ppermute(total, "tgt", swap(k)) for k in (1, 2, 3)]
-    total = (three + one) + (total + two)
+    (a, d, b, c), ends, logs = one_scale(total, three, one, two, 1)
+    total = stacked(24, (d + b) + (a + c), ends, logs)
     one, two, three = [lax.ppermute(total, "tgt", swap(4 * k)) for k in (1, 2, 3)]
-    total = (one + two) + (total + three)
-
-    f_own, v, away = far_pass(order, total, aux, x_sq, tiles)
+    (a, b, c, d), ends, logs = one_scale(total, one, two, three, 4)
+    total = (b + c) + (a + d)
+
+    f_own, v, away = far_pass(order, total, ends, logs, stat, x_sq, tiles)
     from_far = lax.ppermute(away, "src", swap(2))
     part = near_pass(order, v, tiles) + from_far
     part = part[0:4] + lax.ppermute(part[4:8], "src", swap(1))

time: 2200 us -> 2220 us (level)
  blocking collectives: 1100 us -> 818 us
  loops' own time: 767 us -> 987 us
  local copies, waits for them, and re-layouts: 151 us -> 193 us
    pmax x1, blocking collectives: 426 us -> 284 us  [plain_form(): col_high = lax.pmax(col_parts[0], 'src')]
    pmax x1, blocking collectives: 404 us -> 263 us  [plain_form(): row_high = lax.pmax(row_parts[0], 'tgt')]
    another operation x1, loops' own time: 383 us -> 493 us  [plain_form(): row_parts = lax.fori_loop(0, own_count, row_visit_pair, row_start)]
    another operation x1, loops' own time: 383 us -> 493 us  [plain_form(): col_parts = lax.fori_loop(0, own_count, col_visit_pair, col_start)]
    dot_general x152 -> x194, matrix products: 67.8 us -> 87 us  [cross_cost(): lax.dot_general(left_points, right_points, (((0,), (0,)), ((), ())), prec...]
    dynamic_slice x76 -> x97, local copies, waits for them, and re-layouts: 50.5 us -> 64.8 us  [col_visit_pair(): row_id = own_entries[slot_id, 0] % n_tgt]
    dynamic_slice x76 -> x97, local copies, waits for them, and re-layouts: 50.5 us -> 64.8 us  [row_visit_pair(): row_id = own_entries[slot_id, 0] % n_tgt]
  transfers between devices with their start and end apart: 26 -> 26, of which waited for: 13 -> 11; matrix products, arithmetic and copies ran while one was open for 0% -> 0% of each run, Pallas kernels for 0% -> 0%
where the time goes in v1:
time: 2220 us; the launch traced here: 2190 us
  loops' own time  987 us (44%)
  blocking collectives  818 us (37%)
  local copies, waits for them, and re-layouts  193 us (9%)
  matrix products  87 us (4%)
  starting transfers between devices  47.9 us (2%)
    another operation x1, loops' own time, plain_form(): col_parts = lax.fori_loop(0, own_count, col_visit_pair, col_start)  493 us
    another operation x1, loops' own time, plain_form(): row_parts = lax.fori_loop(0, own_count, row_visit_pair, row_start)  493 us
    pmax x1, blocking collectives, plain_form(): col_high = lax.pmax(col_parts[0], 'src')  284 us
    pmax x1, blocking collectives, plain_form(): row_high = lax.pmax(row_parts[0], 'tgt')  263 us
    dot_general x194, matrix products, cross_cost(): lax.dot_general(left_points, right_points, (((0,), (0,)), ((), ())), prec...  87 us
    psum x1, blocking collectives, plain_form(): col_sum = lax.psum(col_parts[1] * jnp.exp(col_parts[0] - col_high), 'src')  85 us
    psum x1, blocking collectives, plain_form(): row_sum = lax.psum(row_parts[1] * jnp.exp(row_parts[0] - row_high), 'tgt')  74.3 us
    dynamic_slice x97, local copies, waits for them, and re-layouts, row_visit_pair(): row_id = own_entries[slot_id, 0] % n_tgt  64.8 us
  transfers between devices with their start and end apart: 26, of which 11 were waited for; matrix products, arithmetic and copies ran while one was open for 0% of the time, Pallas kernels for 0%

profile of v1, /device:TPU:0, one launch (start us, length us, event | category | flops | bytes accessed | tf_op | source)
XLA Modules:
  0.0 2187.9 jit_solution(6896531177340981470)
XLA Ops:
  0.6 1.6 collective-permute-start.1
  2.3 1.9 collective-permute-start
  5.8 1.5 pack.1
  7.2 5.5 collective-permute-start.6
  12.8 1.6 collective-permute-start.3
  15.6 2.8 collective-permute-start.12
  20.5 2.8 collective-permute-done.12.y3
  23.3 2.8 collective-permute-start.5
  26.8 3.2 collective-permute-done.5.x3
  30.0 5.6 row_pass_a.1
  35.6 2.3 row_pass_b.1
  38.2 3.7 collective-permute-start.15
  44.0 3.0 collective-permute-done.14
  48.7 2.9 collective-permute-start.17
  51.6 1.4 collective-permute-done.19
  53.6 3.0 col_pass_a.1
  56.6 6.3 collective-permute-start.20
  63.0 2.7 col_pass_b.1
  67.0 2.6 collective-permute-start.23
  70.9 1.4 collective-permute-start.22
  72.3 2.3 collective-permute-done.24
  77.6 2110.3 %conditional.1 = (f32[256]{0:T(256)}, f32[256]{0:T(256)}) conditional(s32[]{:T(128)} %bitcast.39, (f32[1,256]{1,0:T(1,128)}, f32[256]{0:T(256)S(1)}, f32[1,256]{1,0:T(1,128)S(1)}, f32[8,256]{1,0:T(8,128)S(1)}, f32[1,256]{1,0:T(1,128)S(1)}) %tuple.131, (f32[256]{0:T(256)S(1)}, s32[1]{0:T(128)}, s32[1,128,2]{1,2,0:T(2,128)S(1)}, ...), branch_computations={%region_0.0_spmd, %region_1.16_spmd} | conditional | flops 102804560 | bytes 15752996 | solution.py:488
  77.7 28.8 %all_to_all.8 = f32[16,64,256]{2,1,0:T(8,128)S(1)} all-to-all(f32[16,64,256]{2,1,0:T(8,128)S(1)} %broadcast_in_dim.0), channel_id=1, replica_groups=mesh['src'=16,'tgt'=16] {'tgt'}, dimensions={0} | all-to-all | bytes 2097152 | tf_op jit(solution)/shard_map/cond/branch_1_fun/all_to_all | solution.py:56
  107.6 7.4 all-to-all-start.1
  115.0 52.0 %all-gather = f32[16,1,256]{2,1,0:T(1,128)S(1)} all-gather(f32[1,1,256]{2,1,0:T(1,128)S(1)} %bitcast.101), channel_id=1, replica_groups=mesh['src'=16,'tgt'=16] {'tgt'}, dimensions={0}, use_global_device_ids=true | all-gather | bytes 17408 | tf_op jit(solution)/shard_map/cond/branch_1_fun/all_gather | solution.py:67
  167.0 31.6 %all-gather.1 = f32[16,1,256]{2,1,0:T(1,128)S(1)} all-gather(f32[1,1,256]{2,1,0:T(1,128)S(1)} %bitcast.99), channel_id=1, replica_groups=mesh['src'=16,'tgt'=16] {'src'}, dimensions={0}, use_global_device_ids=true | all-gather | bytes 17408 | tf_op jit(solution)/shard_map/cond/branch_1_fun/all_gather | solution.py:69
  199.1 641.1 %while.26 = (s32[]{:T(128)}, f32[16,256]{1,0:T(8,128)S(1)}, f32[16,256]{1,0:T(8,128)S(1)}, s32[]{:T(128)}, s32[128,2]{0,1:T(2,128)S(1)}, /*index=5*/f32[4096]{0:...) while((s32[]{:T(128)}, f32[16,256]{1,0:T(8,128)S(1)}, ...), condition=%wide.region_7.7_spmd, body=%wide.region_4.6_spmd.sunk | while | flops 50857000 | bytes 678540 | solution.py:95
  840.2 262.5 %pmax.12 = f32[16,256]{1,0:T(8,128)S(1)} all-reduce(f32[16,256]{1,0:T(8,128)S(1)} %get-tuple-element.314), channel_id=1, replica_groups=mesh['src'=16,'tgt'=16] {'tgt'}, use_global_device_ids=true, to_apply=%region_8.8 | all-reduce | flops 4096 | bytes 32768 | tf_op jit(solution)/shard_map/cond/branch_1_fun/pmax | solution.py:96
  1102.7 74.3 %psum.12 = f32[16,256]{1,0:T(8,128)S(1)} all-reduce(f32[16,256]{1,0:T(8,128)S(1)} %exponential_multiply_fusion.1), channel_id=1, replica_groups=mesh['src'=16,'tgt'=16] {'tgt'}, use_global_device_ids=true, to_apply=%region_9.9 | all-reduce | flops 4096 | bytes 32768 | tf_op jit(solution)/shard_map/cond/branch_1_fun/psum | solution.py:97
  1177.0 641.0 %while.27 = (s32[]{:T(128)}, f32[16,256]{1,0:T(8,128)S(1)}, f32[16,256]{1,0:T(8,128)S(1)}, s32[]{:T(128)}, s32[128,2]{0,1:T(2,128)S(1)}, /*index=5*/f32[4096]{0:...) while((s32[]{:T(128)}, f32[16,256]{1,0:T(8,128)S(1)}, ...), condition=%wide.region_13.13_spmd, body=%wide.region_10.12_spmd.sunk | while | flops 50857000 | bytes 678540 | solution.py:113
  1818.7 283.6 %pmax.13 = f32[16,256]{1,0:T(8,128)S(1)} all-reduce(f32[16,256]{1,0:T(8,128)S(1)} %get-tuple-element.317), channel_id=1, replica_groups=mesh['src'=16,'tgt'=16] {'src'}, use_global_device_ids=true, to_apply=%region_14.14 | all-reduce | flops 4096 | bytes 32768 | tf_op jit(solution)/shard_map/cond/branch_1_fun/pmax | solution.py:114
  2102.3 85.0 %psum.13 = f32[16,256]{1,0:T(8,128)S(1)} all-reduce(f32[16,256]{1,0:T(8,128)S(1)} %exponential_multiply_fusion), channel_id=1, replica_groups=mesh['src'=16,'tgt'=16] {'src'}, use_global_device_ids=true, to_apply=%region_15.15 | all-reduce | flops 4096 | bytes 32768 | tf_op jit(solution)/shard_map/cond/branch_1_fun/psum | solution.py:115
  (1843 shorter events, 311.9 us)
Async XLA Ops:
  0.6 12.1 collective-permute-start.1
  2.3 10.5 collective-permute-start
  4.2 8.6 collective-permute-start.2
  7.2 8.4 collective-permute-start.6
  12.8 13.3 collective-permute-start.3
  15.6 7.7 collective-permute-start.12
  18.5 7.6 collective-permute-start.10
  19.5 6.7 collective-permute-start.8
  20.5 6.2 collective-permute-start.7
  23.3 6.7 collective-permute-start.5
  26.1 9.5 collective-permute-start.4
  26.1 3.9 collective-permute-start.13
  26.2 3.8 collective-permute-start.11
  26.7 3.3 collective-permute-start.9
  38.0 5.6 collective-permute-start.16
  38.2 5.8 collective-permute-start.15
  41.9 5.0 collective-permute-start.14
  47.1 5.9 collective-permute-start.19
  48.0 5.0 collective-permute-start.18
  48.7 4.7 collective-permute-start.17
  53.6 24.0 %copy-start = (f32[64,256]{1,0:T(8,128)S(1)}, f32[64,256]{1,0:T(8,128)}, u32[]{:S(2)}) copy-start(f32[64,256]{1,0:T(8,128)} %x_ref.1) | copy-start | bytes 196612
  53.6 24.0 %copy-start.1 = (f32[64,256]{1,0:T(8,128)S(1)}, f32[64,256]{1,0:T(8,128)}, u32[]{:S(2)}) copy-start(f32[64,256]{1,0:T(8,128)} %y_ref.1) | copy-start | bytes 196612
  53.6 24.0 %copy-start.2 = (s32[1,128,2]{1,2,0:T(2,128)S(1)}, s32[1,128,2]{1,2,0:T(2,128)}, u32[]{:S(2)}) copy-start(s32[1,128,2]{1,2,0:T(2,128)} %param.18) | copy-start | bytes 3076
  53.6 24.0 %copy-start.3 = (f32[256]{0:T(256)S(1)}, f32[256]{0:T(256)}, u32[]{:S(2)}) copy-start(f32[256]{0:T(256)} %param.17) | copy-start | bytes 3076
  53.6 24.0 %copy-start.4 = (f32[256]{0:T(256)S(1)}, f32[256]{0:T(256)}, u32[]{:S(2)}) copy-start(f32[256]{0:T(256)} %param.15) | copy-start | bytes 3076
  53.6 24.0 %copy-start.5 = (f32[256]{0:T(256)S(1)}, f32[256]{0:T(256)}, u32[]{:S(2)}) copy-start(f32[256]{0:T(256)} %param.16) | copy-start | bytes 3076
  56.6 9.0 collective-permute-start.20
  65.7 1.3 collective-permute-start.21
  67.0 5.4 collective-permute-start.23
  69.5 5.1 collective-permute-start.24
  70.9 4.8 collective-permute-start.22
  107.6 91.3 %all-to-all-start.1 = ((f32[16,64,256]{2,1,0:T(8,128)}), f32[16,64,256]{2,1,0:T(8,128)S(1)}, u32[]{:S(2)}, u32[]{:S(2)}) async-start(f32[16,64,256]{2,1,0:T(8,128)} %broadcast_in_dim.1), calls=%async_computation.1 | async-start | bytes 2097152 | tf_op jit(solution)/shard_map/cond/branch_1_fun/all_to_all | solution.py:56

commit v2 on v1

--- a/solution.py
+++ b/solution.py
@@ -472,7 +472,7 @@
     one, other, across = [
         lax.ppermute(part[k : k + 1], "src", swap(bits)) for k, bits in ((1, 4), (2, 12), (3, 8))
     ]
-    part = (other + one) + (part[0:1] + across)
+    part = (part[0:1] + one) + (other + across)
     offset = epsilon * ln2 * stat[1] + y_sq.reshape(BLOCK)
     return f_own.reshape(BLOCK), part.reshape(BLOCK), offset
 

time: 2220 us -> 2210 us (level); the launches traced: 2190 us -> 2200 us
  blocking collectives: 818 us -> 964 us
  loops' own time: 987 us -> 885 us
    pmax x1, blocking collectives: 263 us -> 339 us  [plain_form(): row_high = lax.pmax(row_parts[0], 'tgt')]
    pmax x1, blocking collectives: 284 us -> 352 us  [plain_form(): col_high = lax.pmax(col_parts[0], 'src')]
    another operation x1, loops' own time: 493 us -> 443 us  [plain_form(): col_parts = lax.fori_loop(0, own_count, col_visit_pair, col_start)]
    another operation x1, loops' own time: 493 us -> 443 us  [plain_form(): row_parts = lax.fori_loop(0, own_count, row_visit_pair, row_start)]
    dot_general x194 -> x174, matrix products: 87 us -> 78 us  [cross_cost(): lax.dot_general(left_points, right_points, (((0,), (0,)), ((), ())), prec...]
    dynamic_slice x97 -> x87, local copies, waits for them, and re-layouts: 64.8 us -> 58.2 us  [row_visit_pair(): row_id = own_entries[slot_id, 0] % n_tgt]
    dynamic_slice x97 -> x87, local copies, waits for them, and re-layouts: 64.8 us -> 58.2 us  [col_visit_pair(): row_id = own_entries[slot_id, 0] % n_tgt]
  transfers between devices with their start and end apart: 26 -> 26, of which waited for: 11 -> 10; matrix products, arithmetic and copies ran while one was open for 0% -> 0% of each run, Pallas kernels for 0% -> 0%
where the time goes in v2:
time: 2210 us; the launch traced here: 2200 us
  blocking collectives  964 us (44%)
  loops' own time  885 us (40%)
  local copies, waits for them, and re-layouts  173 us (8%)
  matrix products  78 us (4%)
  starting transfers between devices  48.6 us (2%)
    another operation x1, loops' own time, plain_form(): row_parts = lax.fori_loop(0, own_count, row_visit_pair, row_start)  443 us
    another operation x1, loops' own time, plain_form(): col_parts = lax.fori_loop(0, own_count, col_visit_pair, col_start)  443 us
    pmax x1, blocking collectives, plain_form(): col_high = lax.pmax(col_parts[0], 'src')  352 us
    pmax x1, blocking collectives, plain_form(): row_high = lax.pmax(row_parts[0], 'tgt')  339 us
    psum x1, blocking collectives, plain_form(): col_sum = lax.psum(col_parts[1] * jnp.exp(col_parts[0] - col_high), 'src')  84.1 us
    dot_general x174, matrix products, cross_cost(): lax.dot_general(left_points, right_points, (((0,), (0,)), ((), ())), prec...  78 us
    psum x1, blocking collectives, plain_form(): row_sum = lax.psum(row_parts[1] * jnp.exp(row_parts[0] - row_high), 'tgt')  74.2 us
    dynamic_slice x87, local copies, waits for them, and re-layouts, row_visit_pair(): row_id = own_entries[slot_id, 0] % n_tgt  58.2 us
  transfers between devices with their start and end apart: 26, of which 10 were waited for; matrix products, arithmetic and copies ran while one was open for 0% of the time, Pallas kernels for 0%

profile of v2, /device:TPU:0, one launch (start us, length us, event | category | flops | bytes accessed | tf_op | source)
XLA Modules:
  0.0 2202.0 jit_solution(17391301866833389233)
XLA Ops:
  0.6 1.6 collective-permute-start.1
  2.3 1.9 collective-permute-start
  7.2 5.5 collective-permute-start.6
  12.8 1.6 collective-permute-start.3
  15.6 2.8 collective-permute-start.12
  20.5 2.8 collective-permute-done.12.y3
  23.3 2.8 collective-permute-start.5
  26.8 3.2 collective-permute-done.5.x3
  30.0 4.8 row_pass_a.1
  34.8 2.3 row_pass_b.1
  37.1 2.5 collective-permute-start.16
  39.6 5.0 collective-permute-start.15
  44.7 2.1 collective-permute-done.15
  46.7 3.0 collective-permute-done.14
  50.0 4.3 collective-permute-start.17
  56.3 2.8 col_pass_a.1
  59.1 6.2 collective-permute-start.20
  65.3 2.7 col_pass_b.1
  69.3 2.3 collective-permute-start.24
  72.9 1.6 collective-permute-done.24
  74.5 2.0 collective-permute-done.23
  78.3 2123.7 %conditional.1 = (f32[256]{0:T(256)}, f32[256]{0:T(256)}) conditional(s32[]{:T(128)} %bitcast.39, (f32[1,256]{1,0:T(1,128)}, f32[256]{0:T(256)S(1)}, f32[1,256]{1,0:T(1,128)S(1)}, f32[8,256]{1,0:T(8,128)S(1)}, f32[1,256]{1,0:T(1,128)S(1)}) %tuple.131, (f32[256]{0:T(256)S(1)}, s32[1]{0:T(128)}, s32[1,128,2]{1,2,0:T(2,128)S(1)}, ...), branch_computations={%region_0.0_spmd, %region_1.16_spmd} | conditional | flops 102804560 | bytes 15752996 | solution.py:488
  78.4 30.3 %all_to_all.8 = f32[16,64,256]{2,1,0:T(8,128)S(1)} all-to-all(f32[16,64,256]{2,1,0:T(8,128)S(1)} %broadcast_in_dim.0), channel_id=1, replica_groups=mesh['src'=16,'tgt'=16] {'tgt'}, dimensions={0} | all-to-all | bytes 2097152 | tf_op jit(solution)/shard_map/cond/branch_1_fun/all_to_all | solution.py:56
  109.8 6.8 all-to-all-start.1
  116.7 52.0 %all-gather = f32[16,1,256]{2,1,0:T(1,128)S(1)} all-gather(f32[1,1,256]{2,1,0:T(1,128)S(1)} %bitcast.101), channel_id=1, replica_groups=mesh['src'=16,'tgt'=16] {'tgt'}, dimensions={0}, use_global_device_ids=true | all-gather | bytes 17408 | tf_op jit(solution)/shard_map/cond/branch_1_fun/all_gather | solution.py:67
  168.7 31.6 %all-gather.1 = f32[16,1,256]{2,1,0:T(1,128)S(1)} all-gather(f32[1,1,256]{2,1,0:T(1,128)S(1)} %bitcast.99), channel_id=1, replica_groups=mesh['src'=16,'tgt'=16] {'src'}, dimensions={0}, use_global_device_ids=true | all-gather | bytes 17408 | tf_op jit(solution)/shard_map/cond/branch_1_fun/all_gather | solution.py:69
  200.8 575.0 %while.26 = (s32[]{:T(128)}, f32[16,256]{1,0:T(8,128)S(1)}, f32[16,256]{1,0:T(8,128)S(1)}, s32[]{:T(128)}, s32[128,2]{0,1:T(2,128)S(1)}, /*index=5*/f32[4096]{0:...) while((s32[]{:T(128)}, f32[16,256]{1,0:T(8,128)S(1)}, ...), condition=%wide.region_7.7_spmd, body=%wide.region_4.6_spmd.sunk | while | flops 50857000 | bytes 678540 | solution.py:95
  775.8 339.2 %pmax.12 = f32[16,256]{1,0:T(8,128)S(1)} all-reduce(f32[16,256]{1,0:T(8,128)S(1)} %get-tuple-element.314), channel_id=1, replica_groups=mesh['src'=16,'tgt'=16] {'tgt'}, use_global_device_ids=true, to_apply=%region_8.8 | all-reduce | flops 4096 | bytes 32768 | tf_op jit(solution)/shard_map/cond/branch_1_fun/pmax | solution.py:96
  1115.0 74.2 %psum.12 = f32[16,256]{1,0:T(8,128)S(1)} all-reduce(f32[16,256]{1,0:T(8,128)S(1)} %exponential_multiply_fusion.1), channel_id=1, replica_groups=mesh['src'=16,'tgt'=16] {'tgt'}, use_global_device_ids=true, to_apply=%region_9.9 | all-reduce | flops 4096 | bytes 32768 | tf_op jit(solution)/shard_map/cond/branch_1_fun/psum | solution.py:97
  1189.3 575.0 %while.27 = (s32[]{:T(128)}, f32[16,256]{1,0:T(8,128)S(1)}, f32[16,256]{1,0:T(8,128)S(1)}, s32[]{:T(128)}, s32[128,2]{0,1:T(2,128)S(1)}, /*index=5*/f32[4096]{0:...) while((s32[]{:T(128)}, f32[16,256]{1,0:T(8,128)S(1)}, ...), condition=%wide.region_13.13_spmd, body=%wide.region_10.12_spmd.sunk | while | flops 50857000 | bytes 678540 | solution.py:113
  1765.0 352.2 %pmax.13 = f32[16,256]{1,0:T(8,128)S(1)} all-reduce(f32[16,256]{1,0:T(8,128)S(1)} %get-tuple-element.317), channel_id=1, replica_groups=mesh['src'=16,'tgt'=16] {'src'}, use_global_device_ids=true, to_apply=%region_14.14 | all-reduce | flops 4096 | bytes 32768 | tf_op jit(solution)/shard_map/cond/branch_1_fun/pmax | solution.py:114
  2117.3 84.1 %psum.13 = f32[16,256]{1,0:T(8,128)S(1)} all-reduce(f32[16,256]{1,0:T(8,128)S(1)} %exponential_multiply_fusion), channel_id=1, replica_groups=mesh['src'=16,'tgt'=16] {'src'}, use_global_device_ids=true, to_apply=%region_15.15 | all-reduce | flops 4096 | bytes 32768 | tf_op jit(solution)/shard_map/cond/branch_1_fun/psum | solution.py:115
  (1663 shorter events, 279.4 us)
Async XLA Ops:
  0.6 12.1 collective-permute-start.1
  2.3 10.5 collective-permute-start
  4.2 8.6 collective-permute-start.2
  7.2 8.4 collective-permute-start.6
  12.8 13.3 collective-permute-start.3
  15.6 7.7 collective-permute-start.12
  18.5 7.6 collective-permute-start.10
  19.5 6.7 collective-permute-start.8
  20.5 6.2 collective-permute-start.7
  23.3 6.7 collective-permute-start.5
  26.1 8.7 collective-permute-start.4
  26.1 3.9 collective-permute-start.13
  26.2 3.8 collective-permute-start.11
  26.7 3.3 collective-permute-start.9
  37.1 7.5 collective-permute-start.16
  39.6 7.1 collective-permute-start.15
  44.6 5.0 collective-permute-start.14
  49.8 5.7 collective-permute-start.19
  49.9 5.6 collective-permute-start.18
  50.0 6.1 collective-permute-start.17
  56.3 22.0 copy-start
  56.3 22.0 copy-start.1
  56.3 22.0 copy-start.2
  56.3 22.0 copy-start.3
  56.3 22.0 copy-start.4
  56.3 22.0 copy-start.5
  59.1 8.9 collective-permute-start.20
  68.0 1.3 collective-permute-start.21
  69.3 5.2 collective-permute-start.24
  71.6 4.8 collective-permute-start.23
  71.6 4.8 collective-permute-start.22
  109.8 90.7 %all-to-all-start.1 = ((f32[16,64,256]{2,1,0:T(8,128)}), f32[16,64,256]{2,1,0:T(8,128)S(1)}, u32[]{:S(2)}, u32[]{:S(2)}) async-start(f32[16,64,256]{2,1,0:T(8,128)} %broadcast_in_dim.1), calls=%async_computation.1 | async-start | bytes 2097152 | tf_op jit(solution)/shard_map/cond/branch_1_fun/all_to_all | solution.py:56
